TPU v7x, 32 devices: a whole 2x2x4 slice. The times are simulated.
32 devices in a mesh: wide: 16 (over z, y, core), narrow: 2 (over x).
Axes of the slice: x: 2, y: 2, z: 4, core: 2. Of those that a mesh axis runs over, the one named last changes fastest.
Arguments:
- images: bfloat16 [2048, 72, 256], P('wide'), may hold values from -512 to 512
- defocus: float32 [2048], P('wide'), may hold values from 1 to 3
- class_index: int32 [2048], P('wide'), may hold values from 0 to 47
- rotation_index: int32 [2048], P('wide'), may hold values from 0 to 71
- owner_map: int32 [48], replicated, may hold values from 0 to 15, as said below
- roster: int32 [2, 3], replicated, may hold values from 0 to 15, as said below
- ref_store: bfloat16 [16, 2, 8, 72, 256], P('wide', 'narrow'), may hold values from -0.25 to 0.25
Outputs:
- new_references: bfloat16 [16, 2, 4, 72, 256], P('wide', 'narrow')
- log_evidence: float32 [2048], P('wide')
Inputs may be any that keep to these rules, and one draw needn't show every extreme that they name: Each row of roster names 3 different indices. `owner_map`: in each group of 24 consecutive classes, no index is named more than 4 times, and one index is named exactly 4 times.
All inputs are finite; a program needn't handle non-finite values.
Results may differ from a plain program's by a relative error of at most 0.0038.
The roundings to bfloat16 on the way count: a program that leaves them out, or rounds other values in their place, can miss the bound.
Values may be sent and summed in bfloat16 or wider, within the bound.
A program may use at most 128 MiB of HBM per device.

v0:
```python
import functools
import math

import jax
import jax.numpy as jnp
import numpy as np
from jax import lax
from jax.experimental import pallas as pl
from jax.experimental.pallas import tpu as pltpu
from jax.sharding import PartitionSpec as P

CYCLES = 128
ANGLES = 72
STEPS = 3
OWN_MAX = 4
CLS_GRP = 24
SIGMA_ROT = 8
TAU = 1.0
CONTRAST = 0.1
TOP = lax.Precision.HIGHEST
MESH = pl.DeviceIdType.MESH
VMEM_LIMIT = 56 * 1024 * 1024
F32 = jnp.float32
BF16 = jnp.bfloat16
TILE = 16


def up(value, step):
    return -(-value // step) * step


def tables():
    counting = np.arange(ANGLES)
    phase = (counting[:, None] * counting[None, :] % ANGLES) * (2.0 * math.pi / ANGLES)
    return np.cos(phase).astype(np.float32), np.sin(phase).astype(np.float32)


def contrast(defocus_row):
    particles = defocus_row.shape[1]
    defocus = jnp.swapaxes(jnp.broadcast_to(defocus_row, (CYCLES, particles)), 0, 1)
    cycle = lax.broadcasted_iota(jnp.int32, (particles, CYCLES), 1).astype(F32)
    phase_angle = 8.0 * math.pi * defocus * jnp.square((cycle + 1.0) / CYCLES)
    return -jnp.sin(phase_angle) - CONTRAST * jnp.cos(phase_angle)


def high_low(value):
    high = value.astype(BF16).astype(value.dtype)
    return high, value - high


def iota(shape, dimension):
    return lax.broadcasted_iota(jnp.int32, shape, dimension)


def remote(src, dst, send_sem, recv_sem, **target):
    return pltpu.make_async_remote_copy(
        src_ref=src,
        dst_ref=dst,
        send_sem=send_sem,
        recv_sem=recv_sem,
        device_id=target,
        device_id_type=MESH,
    )


def exact(a, b):
    return jnp.dot(a, b, preferred_element_type=F32, precision=TOP)


def kernel(
    wide, narrow, chunk, pieces_each,
    roster_ref, store_ref, img_hbm, defocus_ref, class_ref, rot_ref, owner_ref,
    dft_ref, rdft_ref, turn_ref, tab_ref, back_ref,
    new_ref, ev_ref,
    piece_ref, con_ref, img_ref, spec, got, gath, rr, ct, sc, num, num_got, den, den_got, den_all, top, top_got,
    part_out, part_got, own, pick, slot_out, har,
    i_sem, a_send, a_recv, b_send, b_recv, y_send, y_recv, c_send, c_recv, t_send, t_recv, d_send, d_recv,
    e_send, e_recv, n_send, n_recv, p_send, p_recv, s_send, s_recv,
):
    me = lax.axis_index("wide")
    col = lax.axis_index("narrow")
    chips = wide // 2
    chip, core = me // 2, lax.rem(me, 2)
    sibling = chip * 2 + 1 - core
    particles = con_ref.shape[0]
    block_classes = CLS_GRP // STEPS
    load = pltpu.make_async_copy(img_hbm, img_ref, i_sem.at[0])
    load.start()
    barrier = pltpu.get_barrier_semaphore()
    for d in range(1, wide):
        pl.semaphore_signal(
            barrier, inc=1, device_id={"wide": lax.rem(me + d, wide)}, device_id_type=MESH
        )
    for d in range(1, narrow):
        pl.semaphore_signal(
            barrier, inc=1, device_id={"narrow": lax.rem(col + d, narrow)}, device_id_type=MESH
        )
    rows = ANGLES // pieces_each
    height = piece_ref.shape[1]
    for part in range(pieces_each):
        row, angle = iota((height, ANGLES), 0), iota((height, ANGLES), 1)
        take = ((row + part * rows == angle) & (row < rows)).astype(F32).astype(BF16)
        for slot in range(block_classes):
            piece = jnp.dot(take, store_ref[0, 0, slot], preferred_element_type=F32).astype(BF16)
            for half in range(2):
                piece_ref[(slot * 2 + half) * pieces_each + part] = piece[
                    :, half * CYCLES : (half + 1) * CYCLES
                ]
    pl.semaphore_wait(barrier, wide + narrow - 2)

    first = []
    for d in range(1, wide):
        peer = lax.rem(me + d, wide)
        copy = remote(piece_ref.at[peer], got.at[me], a_send.at[d], a_recv.at[d], wide=peer)
        copy.start()
        first.append(copy)
    got[me] = piece_ref[me]

    con_ref[...] = contrast(defocus_ref[...])
    class_row = lax.broadcasted_iota(jnp.int32, (CLS_GRP, particles), 0) + col * CLS_GRP
    members = (class_row == class_ref[...]).astype(F32)
    squares = jnp.square(con_ref[...])
    den[...] = exact(members, squares)
    den_copy = remote(den, den_got, d_send.at[0], d_recv.at[0], wide=sibling)
    den_copy.start()

    load.wait()
    dft = dft_ref[...]

    def spectra(group, carry):
        reals, imags = [], []
        for pair in range(TILE // 2):
            columns = []
            for which in range(2):
                row = group * TILE + pair * 2 + which
                gain = con_ref[pl.ds(row, 1), :]
                image = img_ref[row].astype(F32)
                columns.append(
                    jnp.concatenate([image[:, :CYCLES] * gain, image[:, CYCLES:] * gain], axis=0)
                )
            packed = jnp.concatenate(columns, axis=1).astype(BF16)
            out = jnp.dot(dft, packed, preferred_element_type=F32)
            for which in range(2):
                lanes = out[:, which * CYCLES : (which + 1) * CYCLES]
                reals.append(lanes[:ANGLES])
                imags.append(lanes[ANGLES:])
        rows = pl.ds(pl.multiple_of(group * TILE, TILE), TILE)
        spec[0:ANGLES, rows, 0:CYCLES] = jnp.swapaxes(jnp.stack(reals), 0, 1).astype(BF16)
        spec[0:ANGLES, rows, CYCLES:] = jnp.swapaxes(jnp.stack(imags), 0, 1).astype(BF16)
        return carry

    groups = particles // TILE
    cuts = [0, groups // 4, groups // 2, groups * 3 // 4, groups]
    lax.fori_loop(cuts[0], cuts[1], spectra, 0)
    if chunk * chips > ANGLES:
        spec[ANGLES:] = jnp.zeros((chunk * chips - ANGLES, particles, 2 * CYCLES), BF16)

    den_copy.wait_recv()
    den_all[0] = den[...] + den_got[...]
    dens = []
    for e in range(1, chips):
        peer = lax.rem(chip + e, chips) * 2 + core
        copy = remote(den_all.at[0], den_all.at[e], e_send.at[e], e_recv.at[e], wide=peer)
        copy.start()
        dens.append(copy)
    for copy in first:
        copy.wait_recv()
    for step in range(STEPS):
        gath[me, step] = got[roster_ref[col, step]]
    outer = chips // 2
    place, inner = chip // 2, lax.rem(chip, 2)
    partner = (place * 2 + 1 - inner) * 2 + core
    second, third, fourth = [], [], []
    for e in range(1, outer):
        peer = (lax.rem(place + e, outer) * 2 + inner) * 2 + core
        copy = remote(gath.at[me], gath.at[me], b_send.at[e], b_recv.at[e], wide=peer)
        copy.start()
        second.append(copy)
    lax.fori_loop(cuts[1], cuts[2], spectra, 0)
    for e in range(outer):
        origin = (lax.rem(place + outer - e, outer) * 2 + inner) * 2 + core
        if e:
            second[e - 1].wait_recv()
        piece = gath.at[origin]
        copy = remote(piece, piece, y_send.at[e], y_recv.at[e], wide=partner)
        copy.start()
        third.append(copy)
        copy = remote(piece, piece, c_send.at[e], c_recv.at[e], wide=sibling)
        copy.start()
        fourth.append(copy)
    lax.fori_loop(cuts[2], cuts[3], spectra, 0)
    for e in range(outer):
        origin = (lax.rem(place + outer - e, outer) * 2 + 1 - inner) * 2 + core
        third[e].wait_recv()
        piece = gath.at[origin]
        copy = remote(piece, piece, c_send.at[outer + e], c_recv.at[outer + e], wide=sibling)
        copy.start()
        fourth.append(copy)
    lax.fori_loop(cuts[3], cuts[4], spectra, 0)

    lanes = OWN_MAX * CLS_GRP
    classes = narrow * CLS_GRP
    source, lane = iota((classes, lanes), 0), iota((classes, lanes), 1)
    spread = (source == col * CLS_GRP + lane % CLS_GRP).astype(F32).astype(BF16)
    owner_row = jnp.broadcast_to(owner_ref[...].astype(F32), (TILE, classes)).astype(BF16)
    owner_row = jnp.dot(owner_row, spread, preferred_element_type=F32)[0:1]
    shape = (wide * TILE, lanes)
    line, lane = iota(shape, 0), iota(shape, 1)
    held = (owner_row == (line // TILE).astype(F32)).astype(F32)
    before, after = iota((lanes, lanes), 0), iota((lanes, lanes), 1)
    counted = (before <= after) & (before // CLS_GRP == after // CLS_GRP)
    rank = jnp.dot(
        held.astype(BF16), counted.astype(F32).astype(BF16), preferred_element_type=F32
    )
    wanted = (rank - 1.0 == (line % OWN_MAX).astype(F32)).astype(F32)
    wanted = wanted * (lane // CLS_GRP == line // OWN_MAX % OWN_MAX).astype(F32)
    pick[...] = (held * wanted).astype(BF16)
    for copy in fourth:
        copy.wait_recv()

    rdft = rdft_ref[...]
    power = []
    for step in range(STEPS):
        reals, imags = [], []
        for pair in range(block_classes // 2):
            columns = []
            for slot in (2 * pair, 2 * pair + 1):
                start = slot * 2 * pieces_each
                columns.append(
                    jnp.concatenate(
                        [gath[start + k, step] for k in range(2 * pieces_each)], axis=0
                    )
                )
            out = jnp.dot(rdft, jnp.concatenate(columns, axis=1), preferred_element_type=F32)
            for which in range(2):
                lanes = out[:, which * CYCLES : (which + 1) * CYCLES]
                reals.append(lanes[:ANGLES])
                imags.append(lanes[ANGLES:])
        real = jnp.swapaxes(jnp.stack(reals), 0, 1).astype(BF16).astype(F32)
        imag = jnp.swapaxes(jnp.stack(imags), 0, 1).astype(BF16).astype(F32)
        power.append(jnp.sum(real * real + imag * imag, axis=0))
        first_rows = jnp.concatenate([real, imag], axis=-1)
        second_rows = jnp.concatenate([-imag, real], axis=-1)
        rr[:, step] = jnp.concatenate([first_rows, second_rows], axis=1).astype(BF16)
    energy = lax.dot_general(
        jnp.concatenate(power, axis=0), squares, (((1,), (1,)), ((), ())),
        preferred_element_type=F32, precision=TOP,
    )

    def correlate(m, carry):
        refs = rr[m].reshape(2 * CLS_GRP, 2 * CYCLES)
        ct[m] = lax.dot_general(
            refs, spec[m], (((1,), (1,)), ((), ())), preferred_element_type=F32
        )
        return carry

    lax.fori_loop(0, ANGLES, correlate, 0, unroll=8)

    angle = lax.broadcasted_iota(jnp.int32, (ANGLES, particles), 0)
    distance = jnp.abs(angle - rot_ref[...])
    distance = jnp.minimum(distance, ANGLES - distance).astype(F32)
    prior = -0.5 * jnp.square(distance / SIGMA_ROT)
    turn = turn_ref[...]
    chosen = jnp.zeros((ANGLES, particles), F32)
    best = None
    for step in range(STEPS):
        start = step * 2 * block_classes
        real = jnp.swapaxes(ct[:, start : start + block_classes, :], 0, 1)
        imag = jnp.swapaxes(ct[:, start + block_classes : start + 2 * block_classes, :], 0, 1)
        for pair in range(block_classes // 2):
            slots = (2 * pair, 2 * pair + 1)
            both = jnp.concatenate(
                [
                    jnp.concatenate([real[s] for s in slots], axis=1),
                    jnp.concatenate([imag[s] for s in slots], axis=1),
                ],
                axis=0,
            )
            high, low = high_low(both)
            both = jnp.concatenate([high, low, high], axis=0).astype(BF16)
            turned = jnp.dot(turn, both, preferred_element_type=F32)
            for which, slot in enumerate(slots):
                c = step * block_classes + slot
                lanes = turned[:, which * particles : (which + 1) * particles]
                scores = (lanes - 0.5 * energy[c : c + 1]) / ANGLES + prior
                sc[c] = scores
                chosen = chosen + members[c : c + 1] * scores
                best = scores if best is None else jnp.maximum(best, scores)
    peak = jnp.max(best, axis=0, keepdims=True)
    total = jnp.zeros((ANGLES, particles), F32)
    for c in range(CLS_GRP):
        total = total + jnp.exp(sc[c] - peak)
    top[0:1] = peak
    top[1:2] = jnp.sum(total, axis=0, keepdims=True)
    tops = []
    for d in range(1, narrow):
        copy = remote(top, top_got.at[d], t_send.at[d], t_recv.at[d], narrow=lax.rem(col + d, narrow))
        copy.start()
        tops.append(copy)
    weight = jnp.exp(chosen - jnp.max(chosen, axis=0, keepdims=True))
    weight = weight / jnp.sum(weight, axis=0, keepdims=True)
    high, low = high_low(weight)
    weight = jnp.swapaxes(jnp.concatenate([high, high, low], axis=0), 0, 1).astype(BF16)
    picked = jnp.concatenate([members, jnp.zeros((8, particles), F32)], axis=0).astype(BF16)

    mine = pl.ds(pl.multiple_of(core * CYCLES, CYCLES), CYCLES)
    theirs = pl.ds(pl.multiple_of((1 - core) * CYCLES, CYCLES), CYCLES)
    flat = chunk * CLS_GRP
    padded = up(flat, 16)
    halves, parts = [], []

    def pass_on(e):
        place = lax.rem(chip + 1 + e, chips)
        rows = pl.ds(place * chunk, chunk)
        halves[e].wait_recv()
        both = num[rows, :, mine] + num_got[rows]
        if e == chips - 1:
            own[...] = both
            return
        both = both.reshape(flat, CYCLES)
        if padded > flat:
            both = jnp.concatenate([both, jnp.zeros((padded - flat, CYCLES), F32)], axis=0)
        part_out[e] = both.astype(BF16)
        copy = remote(
            part_out.at[e], part_got.at[e], p_send.at[e], p_recv.at[e], wide=place * 2 + core
        )
        copy.start()
        parts.append(copy)

    for e in range(chips):
        place = lax.rem(chip + 1 + e, chips)
        coeff = jnp.dot(weight, tab_ref[place], preferred_element_type=F32)
        for row in range(chunk):
            wide_spec = spec[place * chunk + row].astype(F32)
            x_real, x_imag = wide_spec[:, :CYCLES], wide_spec[:, CYCLES:]
            h_real = coeff[:, row : row + 1]
            h_imag = coeff[:, 64 + row : 65 + row]
            a_real = x_real * h_real - x_imag * h_imag
            a_imag = x_real * h_imag + x_imag * h_real
            aligned = jnp.concatenate([a_real, a_imag], axis=-1).astype(BF16)
            sums = jnp.dot(picked, aligned, preferred_element_type=F32)
            num[place * chunk + row] = sums[:CLS_GRP]
        rows = pl.ds(place * chunk, chunk)
        copy = remote(
            num.at[rows, :, theirs], num_got.at[rows], n_send.at[e], n_recv.at[e], wide=sibling
        )
        copy.start()
        halves.append(copy)
        if e:
            pass_on(e - 1)
    pass_on(chips - 1)

    peak, total = top[0:1], top[1:2]
    for d in range(1, narrow):
        tops[d - 1].wait_recv()
        other = top_got[d, 0:1]
        joined = jnp.maximum(peak, other)
        total = total * jnp.exp(peak - joined) + top_got[d, 1:2] * jnp.exp(other - joined)
        peak = joined
    ev_ref[...] = peak + jnp.log(total)
    for copy in dens:
        copy.wait_recv()
    scale = den_all[0]
    for e in range(1, chips):
        scale = scale + den_all[e]
    scale = 1.0 / (scale + TAU)
    for copy in parts:
        copy.wait_recv()
    summed = own[...].reshape(flat, CYCLES)
    for e in range(chips - 1):
        summed = summed + part_got[e].astype(F32)[:flat]
    summed = summed.reshape(chunk, CLS_GRP, CYCLES) * scale[None]
    quads = -(-chunk // OWN_MAX)
    blank = jnp.zeros((CLS_GRP, CYCLES), F32)
    for quad in range(quads):
        four = range(quad * OWN_MAX, (quad + 1) * OWN_MAX)
        four = jnp.concatenate([summed[r] if r < chunk else blank for r in four], axis=0)
        out = jnp.dot(pick[...], four.astype(BF16), preferred_element_type=F32)
        slot_out[:, quad] = out.astype(BF16).reshape(wide, TILE, CYCLES)
    slots = []
    for d in range(1, wide):
        peer = lax.rem(me + d, wide)
        copy = remote(slot_out.at[peer], har.at[core, chip], s_send.at[d], s_recv.at[d], wide=peer)
        copy.start()
        slots.append(copy)
    har[core, chip] = slot_out[me]
    for copy in slots:
        copy.wait_recv()
    length = chips * quads * TILE
    both = jnp.concatenate(
        [har[0].reshape(length, CYCLES), har[1].reshape(length, CYCLES)], axis=1
    )
    out = jnp.dot(back_ref[...], jnp.concatenate([both, both]), preferred_element_type=F32)
    size = OWN_MAX * ANGLES
    by_cos, by_sin = out[:size], out[size:]
    real = by_cos[:, :CYCLES] - by_sin[:, CYCLES:]
    imag = by_cos[:, CYCLES:] + by_sin[:, :CYCLES]
    for slot in range(OWN_MAX):
        span = slice(slot * ANGLES, (slot + 1) * ANGLES)
        new_ref[0, 0, slot, :, :CYCLES] = real[span].astype(BF16)
        new_ref[0, 0, slot, :, CYCLES:] = imag[span].astype(BF16)
    for copy in [den_copy] + first + second + third + fourth + halves + tops + dens + parts + slots:
        copy.wait_send()


def per_device(images, defocus, class_index, rotation_index, owner_map, roster, ref_store):
    wide = lax.axis_size("wide")
    narrow = lax.axis_size("narrow")
    chips = wide // 2
    chunk = -(-ANGLES // chips)
    quads = -(-chunk // OWN_MAX)
    particles = images.shape[0]
    cosines, sines = tables()

    block_classes = ref_store.shape[2]
    pieces_each = max(wide // (2 * block_classes), 1)
    rows = ANGLES // pieces_each
    height = up(rows, 16)

    dft = np.block([[cosines, sines], [-sines, cosines]]).astype(BF16)
    spaced = np.zeros((2 * ANGLES, 2, pieces_each, height), np.float32)
    spaced[..., :rows] = dft.astype(np.float32).reshape(2 * ANGLES, 2, pieces_each, rows)
    rdft = spaced.reshape(2 * ANGLES, -1).astype(BF16)
    turn = np.concatenate([cosines, -sines], axis=1)
    tab = np.zeros((chips, ANGLES, CYCLES), np.float32)
    back = np.zeros((2, OWN_MAX, ANGLES, chips, quads, OWN_MAX, OWN_MAX), np.float32)
    for m in range(ANGLES):
        place, row = divmod(m, chunk)
        tab[place, :, row] = cosines[:, m]
        tab[place, :, 64 + row] = sines[:, m]
        for slot in range(OWN_MAX):
            back[0, slot, :, place, row // OWN_MAX, row % OWN_MAX, slot] = cosines[m] / ANGLES
            back[1, slot, :, place, row // OWN_MAX, row % OWN_MAX, slot] = sines[m] / ANGLES
    back = back.reshape(2 * OWN_MAX * ANGLES, chips * quads * TILE)
    high, low = high_low(back)
    back = np.concatenate([high, low], axis=1).astype(BF16)
    high, low = high_low(turn)
    turn = np.concatenate([high, high, low], axis=1).astype(BF16)
    high, low = high_low(tab)
    tab = np.concatenate([high, low, high], axis=1).astype(BF16)

    vmem = pl.BlockSpec(memory_space=pltpu.VMEM)
    dma = pltpu.SemaphoreType.DMA
    flat = up(chunk * CLS_GRP, 16)
    new, evidence = pl.pallas_call(
        functools.partial(kernel, wide, narrow, chunk, pieces_each),
        out_shape=(
            jax.ShapeDtypeStruct((1, 1, OWN_MAX, ANGLES, 2 * CYCLES), BF16),
            jax.ShapeDtypeStruct((1, particles), F32),
        ),
        in_specs=[
            pl.BlockSpec(memory_space=pltpu.SMEM), vmem, pl.BlockSpec(memory_space=pl.ANY)
        ] + [vmem] * 9,
        out_specs=(vmem, vmem),
        scratch_shapes=[
            pltpu.VMEM((wide, height, CYCLES), BF16),
            pltpu.VMEM((particles, CYCLES), F32),
            pltpu.VMEM((particles, ANGLES, 2 * CYCLES), BF16),
            pltpu.VMEM((chunk * chips, particles, 2 * CYCLES), BF16),
            pltpu.VMEM((wide, height, CYCLES), BF16),
            pltpu.VMEM((wide, STEPS, height, CYCLES), BF16),
            pltpu.VMEM((ANGLES, STEPS, 2 * block_classes, 2 * CYCLES), BF16),
            pltpu.VMEM((ANGLES, 2 * CLS_GRP, particles), F32),
            pltpu.VMEM((CLS_GRP, ANGLES, particles), F32),
            pltpu.VMEM((chunk * chips, CLS_GRP, 2 * CYCLES), F32),
            pltpu.VMEM((chunk * chips, CLS_GRP, CYCLES), F32),
            pltpu.VMEM((CLS_GRP, CYCLES), F32),
            pltpu.VMEM((CLS_GRP, CYCLES), F32),
            pltpu.VMEM((chips, CLS_GRP, CYCLES), F32),
            pltpu.VMEM((8, particles), F32),
            pltpu.VMEM((narrow, 8, particles), F32),
            pltpu.VMEM((chips, flat, CYCLES), BF16),
            pltpu.VMEM((chips, flat, CYCLES), BF16),
            pltpu.VMEM((chunk, CLS_GRP, CYCLES), F32),
            pltpu.VMEM((wide * TILE, OWN_MAX * CLS_GRP), BF16),
            pltpu.VMEM((wide, quads, TILE, CYCLES), BF16),
            pltpu.VMEM((2, chips, quads, TILE, CYCLES), BF16),
            dma((1,)),
            dma((wide,)), dma((wide,)),
            dma((chips,)), dma((chips,)),
            dma((chips,)), dma((chips,)),
            dma((chips,)), dma((chips,)),
            dma((narrow,)), dma((narrow,)),
            dma((1,)), dma((1,)),
            dma((chips,)), dma((chips,)),
            dma((chips,)), dma((chips,)),
            dma((chips,)), dma((chips,)),
            dma((wide,)), dma((wide,)),
        ],
        compiler_params=pltpu.CompilerParams(
            collective_id=0, has_side_effects=True, vmem_limit_bytes=VMEM_LIMIT
        ),
        name="class_averages",
    )(
        roster, ref_store, images, defocus.reshape(1, particles),
        class_index.reshape(1, particles), rotation_index.reshape(1, particles),
        owner_map.reshape(1, narrow * CLS_GRP),
        jnp.asarray(dft), jnp.asarray(rdft), jnp.asarray(turn), jnp.asarray(tab), jnp.asarray(back),
    )
    return new, evidence.reshape(particles)


def solution(mesh):
    in_specs = (
        P("wide", None, None),
        P("wide"),
        P("wide"),
        P("wide"),
        P(),
        P(),
        P("wide", "narrow", None, None, None),
    )
    out_specs = (P("wide", "narrow", None, None, None), P("wide"))
    return jax.shard_map(
        per_device, mesh=mesh, in_specs=in_specs, out_specs=out_specs, check_vma=False
    )
```

profile of v0, /device:TPU:0, one launch (start us, length us, event | category | flops | bytes accessed | tf_op | source)
XLA Modules:
  0.0 61.5 jit_solution(3485764770101034265)
XLA Ops:
  0.6 58.2 %class_averages.1 = (bf16[1,1,4,72,256]{4,3,2,1,0:T(8,128)(2,1)}, f32[1,128]{1,0:T(1,128)}) custom-call(s32[2,3]{1,0:T(2,128)} %roster_ref.1, bf16[1,1,8,72,256]{4,3,2,1,0:T(8,128)(2,1)} %store_ref.1, bf16[128,72,256]{2,1,0:T(8,128)(2,1)} %img_hbm.1, f32[1,128]{1,0:T(1,128)} %bitcast.5, s32[1,128]{1,0:T(1,128)} %bitcast.6, s32[1,128]{1,0:T(1,128)} %bitcast.7, ...), custom_call_target="tpu_custom_call" | custom-call | tf_op jit(solution)/shard_map/class_averages/pallas_call | solution.py:445
  58.8 1.6 %copy.16 = bf16[1,1,4,72,256]{4,3,2,1,0:T(8,128)(2,1)} copy(bf16[1,1,4,72,256]{4,3,2,1,0:T(8,128)(2,1)} %get-tuple-element.8) | data formatting | bytes 294912
  60.4 1.2 %copy.17 = f32[128]{0:T(128)} copy(f32[128]{0:T(128)} %bitcast.9) | data formatting | bytes 1024
where the time goes:
time: 61.7 us; the launch traced here: 61.5 us
  Pallas kernels  58.2 us (94%)
  local copies, waits for them, and re-layouts  2.74 us (4%)
  between operations  0.64 us (1%)
    pallas_call x1, Pallas kernels, per_device(): pl.pallas_call(functools.partial(kernel, wide, narrow, chunk, pieces_each...  58.2 us
    unnamed x2, local copies, waits for them, and re-layouts  2.74 us

commit v1 on v0

--- a/solution.py
+++ b/solution.py
@@ -71,8 +71,8 @@
     wide, narrow, chunk, pieces_each,
     roster_ref, store_ref, img_hbm, defocus_ref, class_ref, rot_ref, owner_ref,
     dft_ref, rdft_ref, turn_ref, tab_ref, back_ref,
-    new_ref, ev_ref,
-    piece_ref, con_ref, img_ref, spec, got, gath, rr, ct, sc, num, num_got, den, den_got, den_all, top, top_got,
+    new_ref, peak_ref, total_ref,
+    piece_ref, con_ref, img_ref, spec, spec_t, coeffs, got, gath, rr, ct, sc, num, num_got, den, den_got, den_all, top, top_got,
     part_out, part_got, own, pick, slot_out, har,
     i_sem, a_send, a_recv, b_send, b_recv, y_send, y_recv, c_send, c_recv, t_send, t_recv, d_send, d_recv,
     e_send, e_recv, n_send, n_recv, p_send, p_recv, s_send, s_recv,
@@ -215,6 +215,12 @@
     wanted = (rank - 1.0 == (line % OWN_MAX).astype(F32)).astype(F32)
     wanted = wanted * (lane // CLS_GRP == line // OWN_MAX % OWN_MAX).astype(F32)
     pick[...] = (held * wanted).astype(BF16)
+
+    def flip(m, carry):
+        spec_t[m] = jnp.swapaxes(spec[m], 0, 1)
+        return carry
+
+    lax.fori_loop(0, ANGLES, flip, 0, unroll=4)
     for copy in fourth:
         copy.wait_recv()
 
@@ -249,9 +255,7 @@
 
     def correlate(m, carry):
         refs = rr[m].reshape(2 * CLS_GRP, 2 * CYCLES)
-        ct[m] = lax.dot_general(
-            refs, spec[m], (((1,), (1,)), ((), ())), preferred_element_type=F32
-        )
+        ct[m] = jnp.dot(refs, spec_t[m], preferred_element_type=F32)
         return carry
 
     lax.fori_loop(0, ANGLES, correlate, 0, unroll=8)
@@ -301,6 +305,9 @@
     weight = weight / jnp.sum(weight, axis=0, keepdims=True)
     high, low = high_low(weight)
     weight = jnp.swapaxes(jnp.concatenate([high, high, low], axis=0), 0, 1).astype(BF16)
+    coeff = jnp.dot(weight, tab_ref[...], preferred_element_type=F32)
+    for place in range(chips):
+        coeffs[place] = coeff[:, place * CYCLES : (place + 1) * CYCLES]
     picked = jnp.concatenate([members, jnp.zeros((8, particles), F32)], axis=0).astype(BF16)
 
     mine = pl.ds(pl.multiple_of(core * CYCLES, CYCLES), CYCLES)
@@ -329,7 +336,7 @@
 
     for e in range(chips):
         place = lax.rem(chip + 1 + e, chips)
-        coeff = jnp.dot(weight, tab_ref[place], preferred_element_type=F32)
+        coeff = coeffs[place]
         for row in range(chunk):
             wide_spec = spec[place * chunk + row].astype(F32)
             x_real, x_imag = wide_spec[:, :CYCLES], wide_spec[:, CYCLES:]
@@ -357,7 +364,8 @@
         joined = jnp.maximum(peak, other)
         total = total * jnp.exp(peak - joined) + top_got[d, 1:2] * jnp.exp(other - joined)
         peak = joined
-    ev_ref[...] = peak + jnp.log(total)
+    peak_ref[...] = peak
+    total_ref[...] = total
     for copy in dens:
         copy.wait_recv()
     scale = den_all[0]
@@ -397,8 +405,8 @@
     imag = by_cos[:, CYCLES:] + by_sin[:, :CYCLES]
     for slot in range(OWN_MAX):
         span = slice(slot * ANGLES, (slot + 1) * ANGLES)
-        new_ref[0, 0, slot, :, :CYCLES] = real[span].astype(BF16)
-        new_ref[0, 0, slot, :, CYCLES:] = imag[span].astype(BF16)
+        new_ref[0, 0, slot, :, :CYCLES] = real[span]
+        new_ref[0, 0, slot, :, CYCLES:] = imag[span]
     for copy in [den_copy] + first + second + third + fourth + halves + tops + dens + parts + slots:
         copy.wait_send()
 
@@ -437,26 +445,30 @@
     high, low = high_low(turn)
     turn = np.concatenate([high, high, low], axis=1).astype(BF16)
     high, low = high_low(tab)
-    tab = np.concatenate([high, low, high], axis=1).astype(BF16)
+    tab = np.concatenate([high, low, high], axis=1).transpose(1, 0, 2).reshape(3 * ANGLES, -1)
+    tab = tab.astype(BF16)
 
     vmem = pl.BlockSpec(memory_space=pltpu.VMEM)
     dma = pltpu.SemaphoreType.DMA
     flat = up(chunk * CLS_GRP, 16)
-    new, evidence = pl.pallas_call(
+    new, peak, total = pl.pallas_call(
         functools.partial(kernel, wide, narrow, chunk, pieces_each),
         out_shape=(
-            jax.ShapeDtypeStruct((1, 1, OWN_MAX, ANGLES, 2 * CYCLES), BF16),
+            jax.ShapeDtypeStruct((1, 1, OWN_MAX, ANGLES, 2 * CYCLES), F32),
+            jax.ShapeDtypeStruct((1, particles), F32),
             jax.ShapeDtypeStruct((1, particles), F32),
         ),
         in_specs=[
             pl.BlockSpec(memory_space=pltpu.SMEM), vmem, pl.BlockSpec(memory_space=pl.ANY)
         ] + [vmem] * 9,
-        out_specs=(vmem, vmem),
+        out_specs=(vmem, vmem, vmem),
         scratch_shapes=[
             pltpu.VMEM((wide, height, CYCLES), BF16),
             pltpu.VMEM((particles, CYCLES), F32),
             pltpu.VMEM((particles, ANGLES, 2 * CYCLES), BF16),
             pltpu.VMEM((chunk * chips, particles, 2 * CYCLES), BF16),
+            pltpu.VMEM((ANGLES, 2 * CYCLES, particles), BF16),
+            pltpu.VMEM((chips, particles, CYCLES), F32),
             pltpu.VMEM((wide, height, CYCLES), BF16),
             pltpu.VMEM((wide, STEPS, height, CYCLES), BF16),
             pltpu.VMEM((ANGLES, STEPS, 2 * block_classes, 2 * CYCLES), BF16),
@@ -497,7 +509,7 @@
         owner_map.reshape(1, narrow * CLS_GRP),
         jnp.asarray(dft), jnp.asarray(rdft), jnp.asarray(turn), jnp.asarray(tab), jnp.asarray(back),
     )
-    return new, evidence.reshape(particles)
+    return new.astype(BF16), (peak + jnp.log(total)).reshape(particles)
 
 
 def solution(mesh):

time: 61.7 us -> 63.2 us (1.024)
  other arithmetic: 0 us -> 2.84 us
  local copies, waits for them, and re-layouts: 2.74 us -> 0 us
  Pallas kernels: 58.2 us -> 59.6 us
    unnamed x2 -> x0, local copies, waits for them, and re-layouts: 2.74 us -> none
    convert_element_type x0 -> x1, other arithmetic: none -> 1.64 us  [per_device(): return (new.astype(BF16), (peak + jnp.log(total)).reshape(particles))]
    pallas_call x1, Pallas kernels: 58.2 us -> 59.6 us  [per_device(): pl.pallas_call(functools.partial(kernel, wide, narrow, chunk, pieces_each...]
    reshape x0 -> x1, other arithmetic: none -> 1.2 us  [per_device(): return (new.astype(BF16), (peak + jnp.log(total)).reshape(particles))]
where the time goes in v1:
time: 63.2 us; the launch traced here: 63 us
  Pallas kernels  59.6 us (94%)
  other arithmetic  2.84 us (4%)
  between operations  0.64 us (1%)
    pallas_call x1, Pallas kernels, per_device(): pl.pallas_call(functools.partial(kernel, wide, narrow, chunk, pieces_each...  59.6 us
    convert_element_type x1, other arithmetic, per_device(): return (new.astype(BF16), (peak + jnp.log(total)).reshape(particles))  1.64 us

profile of v1, /device:TPU:0, one launch (start us, length us, event | category | flops | bytes accessed | tf_op | source)
XLA Modules:
  0.0 63.0 jit_solution(343237464276864660)
XLA Ops:
  0.6 59.6 %class_averages.1 = (f32[1,1,4,72,256]{4,3,2,1,0:T(8,128)}, f32[1,128]{1,0:T(1,128)}, f32[1,128]{1,0:T(1,128)}) custom-call(s32[2,3]{1,0:T(2,128)} %roster_ref.1, bf16[1,1,8,72,256]{4,3,2,1,0:T(8,128)(2,1)} %store_ref.1, bf16[128,72,256]{2,1,0:T(8,128)(2,1)} %img_hbm.1, f32[1,128]{1,0:T(1,128)} %bitcast.6, s32[1,128]{1,0:T(1,128)} %bitcast.7, ...), custom_call_target="tpu_custom_call" | custom-call | tf_op jit(solution)/shard_map/class_averages/pallas_call | solution.py:454
  60.2 1.2 %add_bitcast_fusion = f32[128]{0:T(128)} fusion(f32[1,128]{1,0:T(1,128)} %get-tuple-element.6, f32[1,128]{1,0:T(1,128)} %get-tuple-element.7), kind=kLoop, calls=%fused_computation | loop fusion | flops 128 | bytes 1536 | tf_op jit(solution)/shard_map/reshape | solution.py:512
  61.4 1.6 %convert_element_type.3 = bf16[1,1,4,72,256]{4,3,2,1,0:T(8,128)(2,1)} convert(f32[1,1,4,72,256]{4,3,2,1,0:T(8,128)} %get-tuple-element.5) | non-fusion elementwise | flops 73728 | bytes 442368 | tf_op jit(solution)/shard_map/convert_element_type | solution.py:512

commit v2 on v0

--- a/solution.py
+++ b/solution.py
@@ -72,7 +72,7 @@
     roster_ref, store_ref, img_hbm, defocus_ref, class_ref, rot_ref, owner_ref,
     dft_ref, rdft_ref, turn_ref, tab_ref, back_ref,
     new_ref, ev_ref,
-    piece_ref, con_ref, img_ref, spec, got, gath, rr, ct, sc, num, num_got, den, den_got, den_all, top, top_got,
+    piece_ref, con_ref, img_ref, spec_re, spec_im, coeffs, got, gath, rr_a, rr_b, ct, sc, num, num_got, den, den_got, den_all, top, top_got,
     part_out, part_got, own, pick, slot_out, har,
     i_sem, a_send, a_recv, b_send, b_recv, y_send, y_recv, c_send, c_recv, t_send, t_recv, d_send, d_recv,
     e_send, e_recv, n_send, n_recv, p_send, p_recv, s_send, s_recv,
@@ -83,6 +83,8 @@
     chip, core = me // 2, lax.rem(me, 2)
     sibling = chip * 2 + 1 - core
     particles = con_ref.shape[0]
+    pitch = particles + 8
+    row_pitch = 2 * CLS_GRP + 8
     block_classes = CLS_GRP // STEPS
     load = pltpu.make_async_copy(img_hbm, img_ref, i_sem.at[0])
     load.start()
@@ -128,7 +130,6 @@
     dft = dft_ref[...]
 
     def spectra(group, carry):
-        reals, imags = [], []
         for pair in range(TILE // 2):
             columns = []
             for which in range(2):
@@ -140,20 +141,21 @@
                 )
             packed = jnp.concatenate(columns, axis=1).astype(BF16)
             out = jnp.dot(dft, packed, preferred_element_type=F32)
+            out = out.astype(BF16).astype(F32)
             for which in range(2):
+                row = group * TILE + pair * 2 + which
                 lanes = out[:, which * CYCLES : (which + 1) * CYCLES]
-                reals.append(lanes[:ANGLES])
-                imags.append(lanes[ANGLES:])
-        rows = pl.ds(pl.multiple_of(group * TILE, TILE), TILE)
-        spec[0:ANGLES, rows, 0:CYCLES] = jnp.swapaxes(jnp.stack(reals), 0, 1).astype(BF16)
-        spec[0:ANGLES, rows, CYCLES:] = jnp.swapaxes(jnp.stack(imags), 0, 1).astype(BF16)
+                spec_re[pl.ds(row, ANGLES, stride=pitch), :] = lanes[:ANGLES]
+                spec_im[pl.ds(row, ANGLES, stride=pitch), :] = lanes[ANGLES:]
         return carry
 
     groups = particles // TILE
     cuts = [0, groups // 4, groups // 2, groups * 3 // 4, groups]
     lax.fori_loop(cuts[0], cuts[1], spectra, 0)
     if chunk * chips > ANGLES:
-        spec[ANGLES:] = jnp.zeros((chunk * chips - ANGLES, particles, 2 * CYCLES), BF16)
+        blank = jnp.zeros(((chunk * chips - ANGLES) * pitch, CYCLES), F32)
+        spec_re[ANGLES * pitch :] = blank
+        spec_im[ANGLES * pitch :] = blank
 
     den_copy.wait_recv()
     den_all[0] = den[...] + den_got[...]
@@ -221,7 +223,6 @@
     rdft = rdft_ref[...]
     power = []
     for step in range(STEPS):
-        reals, imags = [], []
         for pair in range(block_classes // 2):
             columns = []
             for slot in (2 * pair, 2 * pair + 1):
@@ -232,25 +233,30 @@
                     )
                 )
             out = jnp.dot(rdft, jnp.concatenate(columns, axis=1), preferred_element_type=F32)
+            out = out.astype(BF16).astype(F32)
             for which in range(2):
+                c = step * block_classes + 2 * pair + which
                 lanes = out[:, which * CYCLES : (which + 1) * CYCLES]
-                reals.append(lanes[:ANGLES])
-                imags.append(lanes[ANGLES:])
-        real = jnp.swapaxes(jnp.stack(reals), 0, 1).astype(BF16).astype(F32)
-        imag = jnp.swapaxes(jnp.stack(imags), 0, 1).astype(BF16).astype(F32)
-        power.append(jnp.sum(real * real + imag * imag, axis=0))
-        first_rows = jnp.concatenate([real, imag], axis=-1)
-        second_rows = jnp.concatenate([-imag, real], axis=-1)
-        rr[:, step] = jnp.concatenate([first_rows, second_rows], axis=1).astype(BF16)
+                real, imag = lanes[:ANGLES], lanes[ANGLES:]
+                power.append(jnp.sum(real * real + imag * imag, axis=0, keepdims=True))
+                plain = pl.ds(c, ANGLES, stride=row_pitch)
+                turned = pl.ds(CLS_GRP + c, ANGLES, stride=row_pitch)
+                rr_a[plain, :] = real
+                rr_b[plain, :] = imag
+                rr_a[turned, :] = -imag
+                rr_b[turned, :] = real
     energy = lax.dot_general(
         jnp.concatenate(power, axis=0), squares, (((1,), (1,)), ((), ())),
         preferred_element_type=F32, precision=TOP,
     )
 
     def correlate(m, carry):
-        refs = rr[m].reshape(2 * CLS_GRP, 2 * CYCLES)
-        ct[m] = lax.dot_general(
-            refs, spec[m], (((1,), (1,)), ((), ())), preferred_element_type=F32
+        rows = pl.ds(pl.multiple_of(m * row_pitch, 8), 2 * CLS_GRP)
+        refs = jnp.concatenate([rr_a[rows, :], rr_b[rows, :]], axis=1).astype(BF16)
+        lines = pl.ds(pl.multiple_of(m * pitch, 8), particles)
+        image = jnp.concatenate([spec_re[lines, :], spec_im[lines, :]], axis=1).astype(BF16)
+        ct[rows, :] = lax.dot_general(
+            refs, image, (((1,), (1,)), ((), ())), preferred_element_type=F32
         )
         return carry
 
@@ -264,15 +270,18 @@
     chosen = jnp.zeros((ANGLES, particles), F32)
     best = None
     for step in range(STEPS):
-        start = step * 2 * block_classes
-        real = jnp.swapaxes(ct[:, start : start + block_classes, :], 0, 1)
-        imag = jnp.swapaxes(ct[:, start + block_classes : start + 2 * block_classes, :], 0, 1)
         for pair in range(block_classes // 2):
             slots = (2 * pair, 2 * pair + 1)
             both = jnp.concatenate(
                 [
-                    jnp.concatenate([real[s] for s in slots], axis=1),
-                    jnp.concatenate([imag[s] for s in slots], axis=1),
+                    jnp.concatenate(
+                        [
+                            ct[pl.ds(half + step * block_classes + s, ANGLES, stride=row_pitch), :]
+                            for s in slots
+                        ],
+                        axis=1,
+                    )
+                    for half in (0, CLS_GRP)
                 ],
                 axis=0,
             )
@@ -301,6 +310,9 @@
     weight = weight / jnp.sum(weight, axis=0, keepdims=True)
     high, low = high_low(weight)
     weight = jnp.swapaxes(jnp.concatenate([high, high, low], axis=0), 0, 1).astype(BF16)
+    coeff = jnp.dot(weight, tab_ref[...], preferred_element_type=F32)
+    for place in range(chips):
+        coeffs[place] = coeff[:, place * CYCLES : (place + 1) * CYCLES]
     picked = jnp.concatenate([members, jnp.zeros((8, particles), F32)], axis=0).astype(BF16)
 
     mine = pl.ds(pl.multiple_of(core * CYCLES, CYCLES), CYCLES)
@@ -329,10 +341,10 @@
 
     for e in range(chips):
         place = lax.rem(chip + 1 + e, chips)
-        coeff = jnp.dot(weight, tab_ref[place], preferred_element_type=F32)
+        coeff = coeffs[place]
         for row in range(chunk):
-            wide_spec = spec[place * chunk + row].astype(F32)
-            x_real, x_imag = wide_spec[:, :CYCLES], wide_spec[:, CYCLES:]
+            lines = pl.ds(pl.multiple_of((place * chunk + row) * pitch, 8), particles)
+            x_real, x_imag = spec_re[lines, :], spec_im[lines, :]
             h_real = coeff[:, row : row + 1]
             h_imag = coeff[:, 64 + row : 65 + row]
             a_real = x_real * h_real - x_imag * h_imag
@@ -437,7 +449,8 @@
     high, low = high_low(turn)
     turn = np.concatenate([high, high, low], axis=1).astype(BF16)
     high, low = high_low(tab)
-    tab = np.concatenate([high, low, high], axis=1).astype(BF16)
+    tab = np.concatenate([high, low, high], axis=1).transpose(1, 0, 2).reshape(3 * ANGLES, -1)
+    tab = tab.astype(BF16)
 
     vmem = pl.BlockSpec(memory_space=pltpu.VMEM)
     dma = pltpu.SemaphoreType.DMA
@@ -456,11 +469,14 @@
             pltpu.VMEM((wide, height, CYCLES), BF16),
             pltpu.VMEM((particles, CYCLES), F32),
             pltpu.VMEM((particles, ANGLES, 2 * CYCLES), BF16),
-            pltpu.VMEM((chunk * chips, particles, 2 * CYCLES), BF16),
+            pltpu.VMEM((chunk * chips * (particles + 8), CYCLES), F32),
+            pltpu.VMEM((chunk * chips * (particles + 8), CYCLES), F32),
+            pltpu.VMEM((chips, particles, CYCLES), F32),
             pltpu.VMEM((wide, height, CYCLES), BF16),
             pltpu.VMEM((wide, STEPS, height, CYCLES), BF16),
-            pltpu.VMEM((ANGLES, STEPS, 2 * block_classes, 2 * CYCLES), BF16),
-            pltpu.VMEM((ANGLES, 2 * CLS_GRP, particles), F32),
+            pltpu.VMEM((ANGLES * (2 * CLS_GRP + 8), CYCLES), F32),
+            pltpu.VMEM((ANGLES * (2 * CLS_GRP + 8), CYCLES), F32),
+            pltpu.VMEM((ANGLES * (2 * CLS_GRP + 8), particles), F32),
             pltpu.VMEM((CLS_GRP, ANGLES, particles), F32),
             pltpu.VMEM((chunk * chips, CLS_GRP, 2 * CYCLES), F32),
             pltpu.VMEM((chunk * chips, CLS_GRP, CYCLES), F32),

time: 61.7 us -> 61.2 us (level)
  no operation moved by 1% of the time
where the time goes in v2:
time: 61.2 us; the launch traced here: 61 us
  Pallas kernels  57.6 us (94%)
  local copies, waits for them, and re-layouts  2.74 us (4%)
  between operations  0.64 us (1%)
    pallas_call x1, Pallas kernels, per_device(): pl.pallas_call(functools.partial(kernel, wide, narrow, chunk, pieces_each...  57.6 us
    unnamed x2, local copies, waits for them, and re-layouts  2.74 us

profile of v2, /device:TPU:0, one launch (start us, length us, event | category | flops | bytes accessed | tf_op | source)
XLA Modules:
  0.0 61.0 jit_solution(8812994364038856081)
XLA Ops:
  0.6 57.6 %class_averages.1 = (bf16[1,1,4,72,256]{4,3,2,1,0:T(8,128)(2,1)}, f32[1,128]{1,0:T(1,128)}) custom-call(s32[2,3]{1,0:T(2,128)} %roster_ref.1, bf16[1,1,8,72,256]{4,3,2,1,0:T(8,128)(2,1)} %store_ref.1, bf16[128,72,256]{2,1,0:T(8,128)(2,1)} %img_hbm.1, f32[1,128]{1,0:T(1,128)} %bitcast.5, s32[1,128]{1,0:T(1,128)} %bitcast.6, s32[1,128]{1,0:T(1,128)} %bitcast.7, ...), custom_call_target="tpu_custom_call" | custom-call | tf_op jit(solution)/shard_map/class_averages/pallas_call | solution.py:458
  58.3 1.6 %copy.16 = bf16[1,1,4,72,256]{4,3,2,1,0:T(8,128)(2,1)} copy(bf16[1,1,4,72,256]{4,3,2,1,0:T(8,128)(2,1)} %get-tuple-element.8) | data formatting | bytes 294912
  59.8 1.2 %copy.17 = f32[128]{0:T(128)} copy(f32[128]{0:T(128)} %bitcast.9) | data formatting | bytes 1024
